TPU v7x, 32 devices: a whole 2x2x4 slice. The times are simulated.
32 devices in a mesh: ctx: 32 (over z, y, x, core).
Axes of the slice: x: 2, y: 2, z: 4, core: 2. Of those that a mesh axis runs over, the one named last changes fastest.
Arguments:
- queries: bfloat16 [16384, 1024], P('ctx'), may hold values from -6 to 6
- key_rows: bfloat16 [16384, 128], P('ctx'), may hold values from -6 to 6
- value_rows: bfloat16 [16384, 128], P('ctx'), may hold values from -6 to 6
- grad_out: bfloat16 [16384, 1024], P('ctx'), may hold values from -16 to 16
- attn_out: bfloat16 [16384, 1024], P('ctx'), may hold values from -6 to 6
- log_total: float32 [8, 16384], P(None, 'ctx'), as said below
- block_pair: int32 [32], P('ctx'), may hold values from 0 to 31, as said below
Outputs:
- grad_queries: bfloat16 [16384, 1024], P('ctx')
- grad_keys: bfloat16 [16384, 128], P('ctx')
- grad_values: bfloat16 [16384, 128], P('ctx')
Inputs may be any that keep to these rules, and one draw needn't show every extreme that they name: `log_total`: the log of the sum of exp(scores) over the visible keys of each head and row. `block_pair`: each block number appears once.
All inputs are finite; a program needn't handle non-finite values.
Results may differ from a plain program's by a relative error of at most 0.0073.
Values may be sent and summed in bfloat16 or wider, within the bound.
A program may use at most 64 MiB of HBM per device.

v0:
```python
import jax
import jax.numpy as jnp
from jax import lax
from jax.sharding import PartitionSpec as P

STEPS = 4


def passed_along(value, axis, steps):
    count = lax.axis_size(axis)
    pairs = [(source, (source + steps) % count) for source in range(count)]
    return lax.ppermute(value, axis, pairs)


def shortened(shard):

    def short(part):
        return part.astype(jnp.bfloat16) if part.dtype == jnp.float32 else part

    return jax.tree.map(short, shard)


def grad_tiles(query_in, grad_in, key_in, value_in, total_in, delta_in, visible, score_scale):
    scores = (
        jnp.einsum("tqhd,tkd->thqk", query_in, key_in, preferred_element_type=jnp.float32)
        * score_scale
    )
    probs = jnp.exp(scores - total_in[..., None])
    if visible is not None:
        probs = jnp.where(visible[:, None], probs, 0.0)
    dprobs = jnp.einsum("tqhd,tkd->thqk", grad_in, value_in, preferred_element_type=jnp.float32)
    dscores = (probs * (dprobs - delta_in[..., None]) * score_scale).astype(jnp.bfloat16)
    probs_b = probs.astype(jnp.bfloat16)
    grad_query = jnp.einsum("thqk,tkd->tqhd", dscores, key_in, preferred_element_type=jnp.float32)
    grad_key = jnp.einsum("thqk,tqhd->tkd", dscores, query_in, preferred_element_type=jnp.float32)
    grad_value = jnp.einsum("thqk,tqhd->tkd", probs_b, grad_in, preferred_element_type=jnp.float32)
    return (grad_query, grad_key, grad_value)


def on_device(queries, key_rows, value_rows, grad_out, attn_out, log_total, block_pair):
    local_rows, head_width = key_rows.shape
    half_rows = local_rows // 2
    head_count = queries.shape[1] // head_width
    cycle_size = lax.axis_size("ctx")
    score_scale = head_width ** (-0.5)
    own_block = block_pair[0]
    offsets = jnp.arange(half_rows, dtype=jnp.int32)

    def places(block):
        return jnp.concatenate(
            [block * half_rows + offsets, (2 * cycle_size - 1 - block) * half_rows + offsets]
        )

    query_pos = places(own_block)
    query_flat = queries.reshape(1, local_rows, head_count, head_width)
    grad_flat = grad_out.reshape(1, local_rows, head_count, head_width)
    query_halves = queries.reshape(2, half_rows, head_count, head_width)
    grad_halves = grad_out.reshape(2, half_rows, head_count, head_width)
    output_rows = attn_out.reshape(local_rows, head_count, head_width)
    visitors = [(key_rows, value_rows, own_block)]
    moving = (key_rows, value_rows, block_pair)
    for step_index in range(1, STEPS):
        moving = passed_along((moving[0], moving[1], moving[2]), "ctx", 1)
        visitors.append((moving[0], moving[1], moving[2][0]))
    delta_flat = jnp.einsum(
        "qhd,qhd->hq", grad_flat[0], output_rows, preferred_element_type=jnp.float32
    )
    total_split = log_total.reshape(head_count, 2, half_rows)
    delta_split = delta_flat.reshape(head_count, 2, half_rows)

    def masked_inputs(visitor):
        key_pos = places(visitor[2])
        visible = (key_pos[None, :] <= query_pos[:, None])[None]
        return (visitor[0][None], visitor[1][None], visible)

    def tile_inputs(visitor):
        earlier = visitor[2] < own_block
        key_halves = visitor[0].reshape(2, half_rows, head_width)
        value_halves = visitor[1].reshape(2, half_rows, head_width)
        query_tile = jnp.stack(
            [query_halves[1], jnp.where(earlier, query_halves[0], query_halves[1])]
        )
        grad_tile = jnp.stack([grad_halves[1], jnp.where(earlier, grad_halves[0], grad_halves[1])])
        key_tile = jnp.stack([key_halves[0], jnp.where(earlier, key_halves[0], key_halves[1])])
        value_tile = jnp.stack(
            [value_halves[0], jnp.where(earlier, value_halves[0], value_halves[1])]
        )
        return (earlier, query_tile, grad_tile, key_tile, value_tile)

    def masked_partial(visitor):
        key_x, value_x, visible = masked_inputs(visitor)
        grad_query, grad_key, grad_value = grad_tiles(
            query_flat,
            grad_flat,
            key_x,
            value_x,
            log_total[None],
            delta_flat[None],
            visible,
            score_scale,
        )
        return (grad_query[0], grad_key[0], grad_value[0])

    def select_partial(visitor):
        earlier, query_tile, grad_tile, key_tile, value_tile = tile_inputs(visitor)
        total_tile = jnp.stack(
            [total_split[:, 1], jnp.where(earlier, total_split[:, 0], total_split[:, 1])]
        )
        delta_tile = jnp.stack(
            [delta_split[:, 1], jnp.where(earlier, delta_split[:, 0], delta_split[:, 1])]
        )
        grad_query, grad_key, grad_value = grad_tiles(
            query_tile, grad_tile, key_tile, value_tile, total_tile, delta_tile, None, score_scale
        )
        query_zero = jnp.zeros_like(grad_query[1])
        key_zero = jnp.zeros_like(grad_key[1])
        query_lower = jnp.where(earlier, grad_query[1], query_zero)
        query_upper = grad_query[0] + jnp.where(earlier, query_zero, grad_query[1])
        key_lower = grad_key[0] + jnp.where(earlier, grad_key[1], key_zero)
        key_upper = jnp.where(earlier, key_zero, grad_key[1])
        value_lower = grad_value[0] + jnp.where(earlier, grad_value[1], key_zero)
        value_upper = jnp.where(earlier, key_zero, grad_value[1])
        return (
            jnp.concatenate([query_lower, query_upper], axis=0),
            jnp.concatenate([key_lower, key_upper], axis=0),
            jnp.concatenate([value_lower, value_upper], axis=0),
        )

    def partial_terms(step_index):
        if step_index > 0:
            return select_partial(visitors[step_index])
        return masked_partial(visitors[step_index])

    grad_query_all = jnp.zeros((local_rows, head_count, head_width), jnp.float32)
    for step_index in range(STEPS):
        query_part, key_part, value_part = partial_terms(step_index)
        grad_query_all = grad_query_all + query_part
        if step_index == 0:
            carried_sums = (key_part, value_part)
        else:
            carried_sums = (carried_sums[0] + key_part, carried_sums[1] + value_part)
        if step_index + 1 < STEPS:
            carried_sums = passed_along((carried_sums[0], carried_sums[1]), "ctx", 1)
    carried_sums = jax.tree.map(
        lambda part, own: part.astype(own.dtype),
        passed_along(shortened(carried_sums), "ctx", 1 - STEPS),
        carried_sums,
    )
    return (
        grad_query_all.reshape(local_rows, head_count * head_width).astype(jnp.bfloat16),
        carried_sums[0].astype(jnp.bfloat16),
        carried_sums[1].astype(jnp.bfloat16),
    )


def solution(mesh):
    return jax.shard_map(
        on_device,
        mesh=mesh,
        in_specs=(
            P("ctx", None),
            P("ctx", None),
            P("ctx", None),
            P("ctx", None),
            P("ctx", None),
            P(None, "ctx"),
            P("ctx"),
        ),
        out_specs=(P("ctx", None), P("ctx", None), P("ctx", None)),
        check_vma=False,
    )
```

profile of v0, /device:TPU:0, one launch (start us, length us, event | category | flops | bytes accessed | tf_op | source)
XLA Modules:
  0.0 133.2 jit_solution(7206068661198958747)
XLA Ops:
  1.2 2.6 %collective-permute-start.2 = (bf16[512,128]{1,0:T(8,128)(2,1)}, bf16[512,128]{1,0:T(8,128)(2,1)S(1)}, u32[]{:S(2)}, u32[]{:S(2)}) collective-permute-start(bf16[512,128]{1,0:T(8,128)(2,1)} %param.9), channel_id=1, source_target_pairs={{0,1},{1,2},{2,3},{3,4},{4,5},{5,6},{6,7},{7,8},{8,9},{9,10},{10,1... | collective-permute-start | bytes 393224 | tf_op jit(solution)/shard_map/ppermute | solution.py:12
  4.7 1.5 %copy.115 = bf16[64,8,8,128]{3,2,1,0:T(8,128)(2,1)S(1)} copy(bf16[64,8,8,128]{3,1,2,0:T(8,128)(2,1)} %bitcast.332) | data formatting | bytes 2097152
  6.2 1.5 %copy.114 = bf16[64,8,8,128]{3,2,1,0:T(8,128)(2,1)S(1)} copy(bf16[64,8,8,128]{3,1,2,0:T(8,128)(2,1)} %bitcast.325) | data formatting | bytes 2097152
  7.7 0.6 fusion.35
  8.5 1.3 fusion.57
  9.8 3.2 %fusion.7 = bf16[8,512,512]{1,2,0:T(8,128)(2,1)S(1)} fusion(f32[512,512,8]{1,0,2:T(8,128)S(1)} %fusion.57, f32[8,512]{1,0:T(8,128)S(1)} %copy.76, f32[8,512]{1,0:T(8,128)S(1)} %copy-done.12, pred[512,512]{0,1:T(8,128)(4,1)S(1)} %broadcast_compare_fusion, bf16[512,128]{1,0:T(8,128)(2,1)S(1)} %copy-done.17, bf16[512,1024]{1,0:T(8,128)(2,1)S(1)} %copy-done.1), kind=kOutput, calls=%fused_computation.9 | convolution fusion | flops 551550976 | bytes 14057472 | tf_op jit(solution)/shard_map/tqhd,tkd->thqk/dot_general | solution.py:31
  13.0 2.0 %convolution_bitcast_fusion.3 = f32[512,128]{1,0:T(8,128)} fusion(bf16[8,512,512]{1,2,0:T(8,128)(2,1)S(1)} %fusion.7, bf16[512,1024]{1,0:T(8,128)(2,1)S(1)} %copy-done), kind=kOutput, calls=%fused_computation.60 | convolution fusion | flops 536870912 | bytes 5505024 | tf_op jit(solution)/shard_map/thqk,tqhd->tkd/dot_general | solution.py:35
  15.0 1.5 %collective-permute-start.9 = (f32[512,128]{1,0:T(8,128)}, f32[512,128]{1,0:T(8,128)}, u32[]{:S(2)}, u32[]{:S(2)}) collective-permute-start(f32[512,128]{1,0:T(8,128)} %convolution_bitcast_fusion.3), channel_id=1, source_target_pairs={{0,1},{1,2},{2,3},{3,4},{4,5},{5,6},{6,7},{7,8},{8,9},{9,10},{10,1... | collective-permute-start | bytes 786440 | tf_op jit(solution)/shard_map/ppermute | solution.py:12
  16.5 2.4 %fusion.51 = f32[512,128]{1,0:T(8,128)} fusion(f32[512,512,8]{1,0,2:T(8,128)S(1)} %fusion.57, f32[8,512]{1,0:T(8,128)S(1)} %copy-done.12, pred[512,512]{0,1:T(8,128)(4,1)S(1)} %broadcast_compare_fusion, bf16[512,1024]{1,0:T(8,128)(2,1)S(1)} %copy-done.1), kind=kOutput, calls=%fused_computation.64 | convolution fusion | flops 545259520 | bytes 9977856 | tf_op jit(solution)/shard_map/thqk,tqhd->tkd/dot_general | solution.py:36
  19.0 0.9 fusion.117
  19.8 1.0 fusion.116
  20.9 0.8 fusion.81
  21.9 1.0 copy.32
  22.9 1.2 copy.108
  24.4 1.2 copy.111
  25.7 1.0 copy.37
  26.7 2.0 %copy.110 = bf16[256,1024]{0,1:T(8,128)(2,1)} copy(bf16[256,1024]{1,0:T(8,128)(2,1)} %get-tuple-element.19) | data formatting | bytes 1048576
  28.7 1.3 copy.39
  30.7 1.6 %collective-permute-start.3 = (s32[1]{0:T(128)}, s32[1]{0:T(128)}, u32[]{:S(2)}, u32[]{:S(2)}) collective-permute-start(s32[1]{0:T(128)} %collective-permute-done), channel_id=1, source_target_pairs={{0,1},{1,2},{2,3},{3,4},{4,5},{5,6},{6,7},{7,8},{8,9},{9,10},{10,1... | collective-permute-start | bytes 20 | tf_op jit(solution)/shard_map/ppermute | solution.py:12
  32.3 5.3 %collective-permute-done.3 = s32[1]{0:T(128)} collective-permute-done((s32[1]{0:T(128)}, s32[1]{0:T(128)}, u32[]{:S(2)}, u32[]{:S(2)}) %collective-permute-start.3) | collective-permute-done | bytes 36 | tf_op jit(solution)/shard_map/ppermute | solution.py:12
  38.5 6.7 %collective-permute-done.6 = s32[1]{0:T(128)} collective-permute-done((s32[1]{0:T(128)}, s32[1]{0:T(128)}, u32[]{:S(2)}, u32[]{:S(2)}) %collective-permute-start.6) | collective-permute-done | bytes 36 | tf_op jit(solution)/shard_map/ppermute | solution.py:12
  45.8 2.7 %broadcast_select_fusion = (bf16[1,256,8,128]{3,1,2,0:T(8,128)(2,1)}, bf16[1,256,8,128]{3,1,2,0:T(8,128)(2,1)}, bf16[1,256,8,128]{3,1,2,0:T(8,128)(2,1)S(1)}, bf...) fusion(bf16[1,256,8,128]{3,1,2,0:T(8,128)(2,1)} %copy.37, ...), kind=kLoop, calls=%fused_computation.84 | loop fusion | flops 1572864 | bytes 5242883 | tf_op jit(solution)/shard_map/jit(_where)/select_n | solution.py:83
  48.4 0.6 pad_maximum_fusion.18
  49.1 0.7 fusion.63
  49.8 1.7 %fusion.42 = f32[2,256,128]{2,1,0:T(8,128)} fusion(f32[2,256,256,8]{2,1,3,0:T(8,128)S(1)} %fusion.63, f32[2,8,256]{2,1,0:T(8,128)S(1)} %get-tuple-element.53, bf16[1,256,8,128]{3,1,2,0:T(8,128)(2,1)S(1)} %copy.39, bf16[1,256,8,128]{3,1,2,0:T(8,128)(2,1)S(1)} %get-tuple-element.14), kind=kOutput, calls=%fused_computation.57 | convolution fusion | flops 272105472 | bytes 5521408 | tf_op jit(solution)/shard_map/thqk,tqhd->tkd/dot_general | solution.py:36
  51.5 0.6 copy-done.8
  52.2 1.3 fusion.18
  53.4 0.7 convolution_bitcast_fusion.6
  54.2 0.9 convolution_bitcast_fusion.2
  55.1 1.5 %slice_select_fusion.2 = (f32[1,256,8,128]{3,1,2,0:T(8,128)}, f32[1,256,8,128]{3,1,2,0:T(8,128)}) fusion(f32[2,256,8,128]{3,1,2,0:T(8,128)S(1)} %convolution_bitcast_fusion.2, pred[]{:T(512)} %bitcast.16), kind=kLoop, calls=%fused_computation.75 | loop fusion | flops 786432 | bytes 4194305 | tf_op jit(solution)/shard_map/jit(_where)/select_n | solution.py:117
  56.6 2.6 %copy.43 = f32[1,256,8,128]{1,3,2,0:T(8,128)} copy(f32[1,256,8,128]{3,1,2,0:T(8,128)} %get-tuple-element.10) | data formatting | bytes 2097152 | tf_op jit(solution)/shard_map/jit(_where)/select_n | solution.py:117
  59.2 0.7 fusion.73
  59.9 2.5 %copy.44 = f32[1,256,8,128]{1,3,2,0:T(8,128)} copy(f32[1,256,8,128]{3,1,2,0:T(8,128)} %get-tuple-element.11) | data formatting | bytes 2097152 | tf_op jit(solution)/shard_map/add | solution.py:118
  62.4 1.0 fusion.70
  63.5 8.5 %collective-permute-done.4 = bf16[512,128]{1,0:T(8,128)(2,1)S(1)} collective-permute-done((bf16[512,128]{1,0:T(8,128)(2,1)}, bf16[512,128]{1,0:T(8,128)(2,1)S(1)}, u32[]{:S(2)}, u32[]{:S(2)}) %collective-permute-start.4) | collective-permute-done | bytes 131104 | tf_op jit(solution)/shard_map/ppermute | solution.py:12
  72.0 1.8 %fusion.64 = f32[2,256,256,8]{2,1,3,0:T(8,128)S(1)} fusion(bf16[1,256,8,128]{3,1,2,0:T(8,128)(2,1)S(1)} %copy.34, bf16[1,256,8,128]{3,1,2,0:T(8,128)(2,1)} %get-tuple-element.59, bf16[1,256,128]{2,1,0:T(8,128)(2,1)S(1)} %get-tuple-element.41, bf16[1,256,128]{2,1,0:T(8,128)(2,1)S(1)} %get-tuple-element.40), kind=kOutput, calls=%fused_computation.81 | convolution fusion | flops 270794752 | bytes 5373952 | tf_op jit(solution)/shard_map/tqhd,tkd->thqk/dot_general | solution.py:25
  73.9 2.4 %fusion.45 = f32[2,256,128]{2,1,0:T(8,128)} fusion(f32[2,256,256,8]{2,1,3,0:T(8,128)S(1)} %fusion.64, f32[2,8,256]{2,1,0:T(8,128)} %get-tuple-element.54, bf16[1,256,8,128]{3,1,2,0:T(8,128)(2,1)S(1)} %copy.39, bf16[1,256,8,128]{3,1,2,0:T(8,128)(2,1)S(1)} %copy-done.6), kind=kOutput, calls=%fused_computation.58 | convolution fusion | flops 272105472 | bytes 5521408 | tf_op jit(solution)/shard_map/thqk,tqhd->tkd/dot_general | solution.py:36
  76.3 0.6 copy-done.10
  77.0 1.2 fusion.14
  78.2 0.9 convolution_bitcast_fusion.1
  79.2 1.6 %slice_select_fusion.1 = (f32[1,256,8,128]{3,1,2,0:T(8,128)}, f32[1,256,8,128]{3,1,2,0:T(8,128)}) fusion(f32[2,256,8,128]{3,1,2,0:T(8,128)S(1)} %convolution_bitcast_fusion.1, pred[]{:T(512)} %bitcast.41), kind=kLoop, calls=%fused_computation.74 | loop fusion | flops 786432 | bytes 4194305 | tf_op jit(solution)/shard_map/jit(_where)/select_n | solution.py:117
  80.7 1.4 %convolution_bitcast_fusion.5 = f32[2,256,128]{2,1,0:T(8,128)} fusion(bf16[2,8,256,256]{2,3,1,0:T(8,128)(2,1)S(1)} %fusion.14, bf16[1,256,8,128]{3,1,2,0:T(8,128)(2,1)S(1)} %copy.34, bf16[1,256,8,128]{3,1,2,0:T(8,128)(2,1)S(1)} %copy-done.3), kind=kOutput, calls=%fused_computation.62 | convolution fusion | flops 268959744 | bytes 3407872 | tf_op jit(solution)/shard_map/thqk,tqhd->tkd/dot_general | solution.py:35
  82.2 1.7 %maximum_add_fusion.1 = f32[512,128]{1,0:T(8,128)} fusion(f32[512,128]{1,0:T(8,128)} %collective-permute-done.9, f32[256,128]{1,0:T(8,128)S(1)} %copy-done.7, f32[256,128]{1,0:T(8,128)S(1)} %get-tuple-element.32), kind=kLoop, calls=%fused_computation.90 | loop fusion | flops 131072 | bytes 786432 | tf_op jit(solution)/shard_map/add | solution.py:141
  83.8 2.5 %copy.54 = f32[1,256,8,128]{1,3,2,0:T(8,128)} copy(f32[1,256,8,128]{3,1,2,0:T(8,128)} %get-tuple-element.8) | data formatting | bytes 2097152 | tf_op jit(solution)/shard_map/jit(_where)/select_n | solution.py:117
  86.4 2.5 %copy.55 = f32[1,256,8,128]{1,3,2,0:T(8,128)} copy(f32[1,256,8,128]{3,1,2,0:T(8,128)} %get-tuple-element.9) | data formatting | bytes 2097152 | tf_op jit(solution)/shard_map/add | solution.py:118
  88.9 1.0 fusion.72
  90.0 1.0 maximum_add_fusion.4
  91.4 1.0 fusion.69
  92.4 11.8 %collective-permute-done.7 = bf16[512,128]{1,0:T(8,128)(2,1)S(1)} collective-permute-done((bf16[512,128]{1,0:T(8,128)(2,1)}, bf16[512,128]{1,0:T(8,128)(2,1)S(1)}, u32[]{:S(2)}, u32[]{:S(2)}) %collective-permute-start.7) | collective-permute-done | bytes 131104 | tf_op jit(solution)/shard_map/ppermute | solution.py:12
  104.1 1.8 %fusion.65 = f32[2,256,256,8]{2,1,3,0:T(8,128)S(1)} fusion(bf16[1,256,8,128]{3,1,2,0:T(8,128)(2,1)S(1)} %copy.34, bf16[1,256,8,128]{3,1,2,0:T(8,128)(2,1)} %get-tuple-element.60, bf16[1,256,128]{2,1,0:T(8,128)(2,1)S(1)} %get-tuple-element.37, bf16[1,256,128]{2,1,0:T(8,128)(2,1)S(1)} %get-tuple-element.36), kind=kOutput, calls=%fused_computation.82 | convolution fusion | flops 270794752 | bytes 5373952 | tf_op jit(solution)/shard_map/tqhd,tkd->thqk/dot_general | solution.py:25
  105.9 1.0 fusion.48
  106.9 1.3 fusion.10
  108.2 0.9 convolution_bitcast_fusion
  109.1 1.5 %slice_select_fusion = (f32[1,256,8,128]{3,1,2,0:T(8,128)}, f32[1,256,8,128]{3,1,2,0:T(8,128)}) fusion(f32[2,256,8,128]{3,1,2,0:T(8,128)S(1)} %convolution_bitcast_fusion, pred[]{:T(512)} %bitcast.56), kind=kLoop, calls=%fused_computation.73 | loop fusion | flops 786432 | bytes 4194305 | tf_op jit(solution)/shard_map/jit(_where)/select_n | solution.py:117
  110.7 0.7 convolution_bitcast_fusion.4
  111.7 2.5 %copy.65 = f32[1,256,8,128]{1,3,2,0:T(8,128)} copy(f32[1,256,8,128]{3,1,2,0:T(8,128)} %get-tuple-element.6) | data formatting | bytes 2097152 | tf_op jit(solution)/shard_map/jit(_where)/select_n | solution.py:117
  114.2 2.6 %copy.66 = f32[1,256,8,128]{1,3,2,0:T(8,128)} copy(f32[1,256,8,128]{3,1,2,0:T(8,128)} %get-tuple-element.7) | data formatting | bytes 2097152 | tf_op jit(solution)/shard_map/add | solution.py:118
  116.8 4.2 %collective-permute-done.11 = f32[512,128]{1,0:T(8,128)S(1)} collective-permute-done((f32[512,128]{1,0:T(8,128)S(1)}, f32[512,128]{1,0:T(8,128)S(1)}, u32[]{:S(2)}, u32[]{:S(2)}) %collective-permute-start.11) | collective-permute-done | bytes 262176 | tf_op jit(solution)/shard_map/ppermute | solution.py:12
  121.1 2.8 %collective-permute-done.15 = f32[512,128]{1,0:T(8,128)} collective-permute-done((f32[512,128]{1,0:T(8,128)S(1)}, f32[512,128]{1,0:T(8,128)}, u32[]{:S(2)}, u32[]{:S(2)}) %collective-permute-start.15) | collective-permute-done | bytes 262176 | tf_op jit(solution)/shard_map/ppermute | solution.py:12
  123.9 1.0 fusion.67
  125.0 4.6 %fusion.34 = bf16[512,1024]{0,1:T(8,128)(2,1)} fusion(f32[256,1024]{0,1:T(8,128)} %bitcast.320, f32[256,1024]{0,1:T(8,128)} %bitcast.319, f32[256,1024]{0,1:T(8,128)} %bitcast.322, f32[256,1024]{0,1:T(8,128)} %bitcast.321, f32[256,1024]{0,1:T(8,128)} %bitcast.324, f32[256,1024]{0,1:T(8,128)} %bitcast.323, f32[8,512,128]{1,2,0:T(8,128)S(1)} %fusion.81), kind=kLoop, calls=%fused_computation.39 | loop fusion | flops 3670016 | bytes 9437184 | tf_op jit(solution)/shard_map/convert_element_type | solution.py:150
  129.6 2.3 %copy.69 = bf16[512,1024]{1,0:T(8,128)(2,1)} copy(bf16[512,1024]{0,1:T(8,128)(2,1)} %fusion.34) | data formatting | bytes 2097152
  131.8 0.7 copy.135
  132.5 0.7 copy.136
  (80 shorter events, 2.6 us)
Async XLA Ops:
  0.6 7.8 %copy-start.4 = (bf16[512,128]{1,0:T(8,128)(2,1)S(1)}, bf16[512,128]{1,0:T(8,128)(2,1)}, u32[]{:S(2)}) copy-start(bf16[512,128]{1,0:T(8,128)(2,1)} %param.8) | copy-start | bytes 393220
  0.6 7.8 %copy-start = (bf16[512,1024]{1,0:T(8,128)(2,1)S(1)}, bf16[512,1024]{1,0:T(8,128)(2,1)}, u32[]{:S(2)}) copy-start(bf16[512,1024]{1,0:T(8,128)(2,1)} %param.7) | copy-start | bytes 3145732
  0.7 29.4 %collective-permute-start = (s32[1]{0:T(128)}, s32[1]{0:T(128)}, u32[]{:S(2)}, u32[]{:S(2)}) collective-permute-start(s32[1]{0:T(128)} %param.13), channel_id=1, source_target_pairs={{0,1},{1,2},{2,3},{3,4},{4,5},{5,6},{6,7},{7,8},{8,9},{9,10},{10,1... | collective-permute-start | bytes 20 | tf_op jit(solution)/shard_map/ppermute | solution.py:12
  1.2 50.4 %collective-permute-start.2 = (bf16[512,128]{1,0:T(8,128)(2,1)}, bf16[512,128]{1,0:T(8,128)(2,1)S(1)}, u32[]{:S(2)}, u32[]{:S(2)}) collective-permute-start(bf16[512,128]{1,0:T(8,128)(2,1)} %param.9), channel_id=1, source_target_pairs={{0,1},{1,2},{2,3},{3,4},{4,5},{5,6},{6,7},{7,8},{8,9},{9,10},{10,1... | collective-permute-start | bytes 393224 | tf_op jit(solution)/shard_map/ppermute | solution.py:12
  3.8 45.3 %collective-permute-start.1 = (bf16[512,128]{1,0:T(8,128)(2,1)}, bf16[512,128]{1,0:T(8,128)(2,1)S(1)}, u32[]{:S(2)}, u32[]{:S(2)}) collective-permute-start(bf16[512,128]{1,0:T(8,128)(2,1)} %param.8), channel_id=1, source_target_pairs={{0,1},{1,2},{2,3},{3,4},{4,5},{5,6},{6,7},{7,8},{8,9},{9,10},{10,1... | collective-permute-start | bytes 393224 | tf_op jit(solution)/shard_map/ppermute | solution.py:12
  8.5 1.3 copy-start.1
  8.5 1.3 copy-start.12
  8.5 1.3 copy-start.17
  15.0 67.2 %collective-permute-start.9 = (f32[512,128]{1,0:T(8,128)}, f32[512,128]{1,0:T(8,128)}, u32[]{:S(2)}, u32[]{:S(2)}) collective-permute-start(f32[512,128]{1,0:T(8,128)} %convolution_bitcast_fusion.3), channel_id=1, source_target_pairs={{0,1},{1,2},{2,3},{3,4},{4,5},{5,6},{6,7},{7,8},{8,9},{9,10},{10,1... | collective-permute-start | bytes 786440 | tf_op jit(solution)/shard_map/ppermute | solution.py:12
  18.9 71.1 %collective-permute-start.13 = (f32[512,128]{1,0:T(8,128)}, f32[512,128]{1,0:T(8,128)}, u32[]{:S(2)}, u32[]{:S(2)}) collective-permute-start(f32[512,128]{1,0:T(8,128)} %fusion.51), channel_id=1, source_target_pairs={{0,1},{1,2},{2,3},{3,4},{4,5},{5,6},{6,7},{7,8},{8,9},{9,10},{10,1... | collective-permute-start | bytes 786440 | tf_op jit(solution)/shard_map/ppermute | solution.py:12
  21.7 24.1 %copy-start.13 = (f32[8,512]{1,0:T(8,128)S(1)}, f32[8,512]{1,0:T(8,128)}, u32[]{:S(2)}) copy-start(f32[8,512]{1,0:T(8,128)} %param.12) | copy-start | bytes 49156
  30.7 6.9 %collective-permute-start.3 = (s32[1]{0:T(128)}, s32[1]{0:T(128)}, u32[]{:S(2)}, u32[]{:S(2)}) collective-permute-start(s32[1]{0:T(128)} %collective-permute-done), channel_id=1, source_target_pairs={{0,1},{1,2},{2,3},{3,4},{4,5},{5,6},{6,7},{7,8},{8,9},{9,10},{10,1... | collective-permute-start | bytes 20 | tf_op jit(solution)/shard_map/ppermute | solution.py:12
  38.2 7.0 %collective-permute-start.6 = (s32[1]{0:T(128)}, s32[1]{0:T(128)}, u32[]{:S(2)}, u32[]{:S(2)}) collective-permute-start(s32[1]{0:T(128)} %collective-permute-done.3), channel_id=1, source_target_pairs={{0,1},{1,2},{2,3},{3,4},{4,5},{5,6},{6,7},{7,8},{8,9},{9,10},{10,1... | collective-permute-start | bytes 20 | tf_op jit(solution)/shard_map/ppermute | solution.py:12
  49.1 2.4 %copy-start.9 = (bf16[512,128]{1,0:T(8,128)(2,1)}, bf16[512,128]{1,0:T(8,128)(2,1)S(1)}, u32[]{:S(2)}) copy-start(bf16[512,128]{1,0:T(8,128)(2,1)S(1)} %collective-permute-done.1) | copy-start | bytes 393220
  51.5 0.7 copy-start.8
  62.4 11.4 %copy-start.6 = (bf16[1,256,8,128]{3,1,2,0:T(8,128)(2,1)S(1)}, bf16[1,256,8,128]{3,1,2,0:T(8,128)(2,1)}, u32[]{:S(2)}) copy-start(bf16[1,256,8,128]{3,1,2,0:T(8,128)(2,1)} %get-tuple-element.13) | copy-start | bytes 1572868
  62.4 13.9 %collective-permute-start.5 = (bf16[512,128]{1,0:T(8,128)(2,1)}, bf16[512,128]{1,0:T(8,128)(2,1)S(1)}, u32[]{:S(2)}, u32[]{:S(2)}) collective-permute-start(bf16[512,128]{1,0:T(8,128)(2,1)} %copy-done.8), channel_id=1, source_target_pairs={{0,1},{1,2},{2,3},{3,4},{4,5},{5,6},{6,7},{7,8},{8,9},{9,10},{10,1... | collective-permute-start | bytes 393224 | tf_op jit(solution)/shard_map/ppermute | solution.py:12
  62.4 9.6 %collective-permute-start.4 = (bf16[512,128]{1,0:T(8,128)(2,1)}, bf16[512,128]{1,0:T(8,128)(2,1)S(1)}, u32[]{:S(2)}, u32[]{:S(2)}) collective-permute-start(bf16[512,128]{1,0:T(8,128)(2,1)} %copy-done.9), channel_id=1, source_target_pairs={{0,1},{1,2},{2,3},{3,4},{4,5},{5,6},{6,7},{7,8},{8,9},{9,10},{10,1... | collective-permute-start | bytes 393224 | tf_op jit(solution)/shard_map/ppermute | solution.py:12
  72.0 4.3 %copy-start.11 = (bf16[512,128]{1,0:T(8,128)(2,1)}, bf16[512,128]{1,0:T(8,128)(2,1)S(1)}, u32[]{:S(2)}) copy-start(bf16[512,128]{1,0:T(8,128)(2,1)S(1)} %collective-permute-done.4) | copy-start | bytes 393220
  73.8 3.1 %copy-start.15 = (f32[2,8,256]{2,1,0:T(8,128)S(1)}, f32[2,8,256]{2,1,0:T(8,128)}, u32[]{:S(2)}) copy-start(f32[2,8,256]{2,1,0:T(8,128)} %get-tuple-element.54) | copy-start | bytes 49156
  73.8 3.1 %copy-start.16 = (f32[2,8,256]{2,1,0:T(8,128)S(1)}, f32[2,8,256]{2,1,0:T(8,128)}, u32[]{:S(2)}) copy-start(f32[2,8,256]{2,1,0:T(8,128)} %get-tuple-element.61) | copy-start | bytes 49156
  76.3 0.7 copy-start.10
  78.2 2.5 %copy-start.3 = (bf16[1,256,8,128]{3,1,2,0:T(8,128)(2,1)S(1)}, bf16[1,256,8,128]{3,1,2,0:T(8,128)(2,1)}, u32[]{:S(2)}) copy-start(bf16[1,256,8,128]{3,1,2,0:T(8,128)(2,1)} %get-tuple-element.59) | copy-start | bytes 1572868
  79.2 3.0 %copy-start.7 = (f32[256,128]{1,0:T(8,128)S(1)}, f32[256,128]{1,0:T(8,128)}, u32[]{:S(2)}) copy-start(f32[256,128]{1,0:T(8,128)} %get-tuple-element.33) | copy-start | bytes 393220
  88.9 17.0 %copy-start.5 = (bf16[1,256,8,128]{3,1,2,0:T(8,128)(2,1)S(1)}, bf16[1,256,8,128]{3,1,2,0:T(8,128)(2,1)}, u32[]{:S(2)}) copy-start(bf16[1,256,8,128]{3,1,2,0:T(8,128)(2,1)} %get-tuple-element.12) | copy-start | bytes 1572868
  88.9 22.5 %collective-permute-start.10 = (f32[512,128]{1,0:T(8,128)}, f32[512,128]{1,0:T(8,128)S(1)}, u32[]{:S(2)}, u32[]{:S(2)}) collective-permute-start(f32[512,128]{1,0:T(8,128)} %maximum_add_fusion.1), channel_id=1, source_target_pairs={{0,1},{1,2},{2,3},{3,4},{4,5},{5,6},{6,7},{7,8},{8,9},{9,10},{10,1... | collective-permute-start | bytes 786440 | tf_op jit(solution)/shard_map/ppermute | solution.py:12
  90.9 20.6 %collective-permute-start.14 = (f32[512,128]{1,0:T(8,128)S(1)}, f32[512,128]{1,0:T(8,128)S(1)}, u32[]{:S(2)}, u32[]{:S(2)}) collective-permute-start(f32[512,128]{1,0:T(8,128)S(1)} %maximum_add_fusion.4), channel_id=1, source_target_pairs={{0,1},{1,2},{2,3},{3,4},{4,5},{5,6},{6,7},{7,8},{8,9},{9,10},{10,1... | collective-permute-start | bytes 786440 | tf_op jit(solution)/shard_map/ppermute | solution.py:12
  91.0 15.9 %collective-permute-start.8 = (bf16[512,128]{1,0:T(8,128)(2,1)}, bf16[512,128]{1,0:T(8,128)(2,1)S(1)}, u32[]{:S(2)}, u32[]{:S(2)}) collective-permute-start(bf16[512,128]{1,0:T(8,128)(2,1)} %copy-done.10), channel_id=1, source_target_pairs={{0,1},{1,2},{2,3},{3,4},{4,5},{5,6},{6,7},{7,8},{8,9},{9,10},{10,1... | collective-permute-start | bytes 393224 | tf_op jit(solution)/shard_map/ppermute | solution.py:12
  91.1 13.0 %collective-permute-start.7 = (bf16[512,128]{1,0:T(8,128)(2,1)}, bf16[512,128]{1,0:T(8,128)(2,1)S(1)}, u32[]{:S(2)}, u32[]{:S(2)}) collective-permute-start(bf16[512,128]{1,0:T(8,128)(2,1)} %copy-done.11), channel_id=1, source_target_pairs={{0,1},{1,2},{2,3},{3,4},{4,5},{5,6},{6,7},{7,8},{8,9},{9,10},{10,1... | collective-permute-start | bytes 393224 | tf_op jit(solution)/shard_map/ppermute | solution.py:12
  105.9 1.0 copy-start.14
  108.2 2.5 %copy-start.2 = (bf16[1,256,8,128]{3,1,2,0:T(8,128)(2,1)S(1)}, bf16[1,256,8,128]{3,1,2,0:T(8,128)(2,1)}, u32[]{:S(2)}) copy-start(bf16[1,256,8,128]{3,1,2,0:T(8,128)(2,1)} %get-tuple-element.60) | copy-start | bytes 1572868
  111.5 9.5 %collective-permute-start.11 = (f32[512,128]{1,0:T(8,128)S(1)}, f32[512,128]{1,0:T(8,128)S(1)}, u32[]{:S(2)}, u32[]{:S(2)}) collective-permute-start(f32[512,128]{1,0:T(8,128)S(1)} %maximum_add_fusion.2), channel_id=1, source_target_pairs={{0,1},{1,2},{2,3},{3,4},{4,5},{5,6},{6,7},{7,8},{8,9},{9,10},{10,1... | collective-permute-start | bytes 786440 | tf_op jit(solution)/shard_map/ppermute | solution.py:12
  111.6 12.3 %collective-permute-start.15 = (f32[512,128]{1,0:T(8,128)S(1)}, f32[512,128]{1,0:T(8,128)}, u32[]{:S(2)}, u32[]{:S(2)}) collective-permute-start(f32[512,128]{1,0:T(8,128)S(1)} %maximum_add_fusion.5), channel_id=1, source_target_pairs={{0,1},{1,2},{2,3},{3,4},{4,5},{5,6},{6,7},{7,8},{8,9},{9,10},{10,1... | collective-permute-start | bytes 786440 | tf_op jit(solution)/shard_map/ppermute | solution.py:12
  121.0 10.8 %collective-permute-start.12 = (bf16[512,128]{1,0:T(8,128)(2,1)S(1)}, bf16[512,128]{1,0:T(8,128)(2,1)S(1)}, u32[]{:S(2)}, u32[]{:S(2)}) collective-permute-start(bf16[512,128]{1,0:T(8,128)(2,1)S(1)} %fusion.66), channel_id=1, source_target_pairs={{0,29},{1,30},{2,31},{3,0},{4,1},{5,2},{6,3},{7,4},{8,5},{9,6},{10... | collective-permute-start | bytes 393224 | tf_op jit(solution)/shard_map/ppermute | solution.py:12
  124.9 6.9 %collective-permute-start.16 = (bf16[512,128]{1,0:T(8,128)(2,1)S(1)}, bf16[512,128]{1,0:T(8,128)(2,1)S(1)}, u32[]{:S(2)}, u32[]{:S(2)}) collective-permute-start(bf16[512,128]{1,0:T(8,128)(2,1)S(1)} %fusion.67), channel_id=1, source_target_pairs={{0,29},{1,30},{2,31},{3,0},{4,1},{5,2},{6,3},{7,4},{8,5},{9,6},{10... | collective-permute-start | bytes 393224 | tf_op jit(solution)/shard_map/ppermute | solution.py:12
where the time goes:
time: 134 us; the launch traced here: 133 us
  waiting for transfers between devices  39.4 us (29%)
  local copies, waits for them, and re-layouts  33.5 us (25%)
  matrix products  28.3 us (21%)
  other arithmetic  21 us (16%)
  starting transfers between devices  7.25 us (5%)
  between operations  3.66 us (3%)
    ppermute x17, waiting for transfers between devices, passed_along(): return lax.ppermute(value, axis, pairs)  39.4 us
    unnamed x45, local copies, waits for them, and re-layouts  12.6 us
    select_n x3, local copies, waits for them, and re-layouts, select_partial(): query_lower = jnp.where(earlier, grad_query[1], query_zero)  7.62 us
    add x3, local copies, waits for them, and re-layouts, select_partial(): query_upper = grad_query[0] + jnp.where(earlier, query_zero, grad_query[1])  7.61 us
    dot_general x4, matrix products, grad_tiles(): jnp.einsum('thqk,tqhd->tkd', probs_b, grad_in, preferred_element_type=jnp...  7.45 us
    ppermute x17, starting transfers between devices, passed_along(): return lax.ppermute(value, axis, pairs)  7.25 us
    dot_general x4, matrix products, grad_tiles(): jnp.einsum('tqhd,tkd->thqk', grad_in, value_in, preferred_element_type=jn...  7.01 us
    dot_general x4, matrix products, grad_tiles(): jnp.einsum('tqhd,tkd->thqk', query_in, key_in, preferred_element_type=jnp...  5.51 us
  transfers between devices with their start and end apart: 17, of which 6 were waited for; matrix products, arithmetic and copies ran while one was open for 60% of the time, Pallas kernels for 0%

commit v1 on v0

v1 whole, which is shorter than its diff:
```python
import functools
import math

import jax
import jax.numpy as jnp
from jax import lax
from jax.experimental import pallas as pl
from jax.experimental.pallas import tpu as pltpu
from jax.sharding import PartitionSpec as P

MESH = pl.DeviceIdType.MESH
LOG2E = math.log2(math.e)
F32 = jnp.float32
BF16 = jnp.bfloat16
UNROLL = 2


def dot_nt(a, b):
    return lax.dot_general(a, b, (((1,), (1,)), ((), ())), preferred_element_type=F32)


def dot_nn(a, b):
    return jnp.dot(a, b, preferred_element_type=F32)


def kernel(
    count, heads, tile_ref, q_hbm, k_hbm, v_hbm, g_hbm, o_hbm, l_hbm,
    gq_hbm, gk_ref, gv_ref,
    q_s, g_s, o_s, l_s, d_s, dq_s, gq_s,
    k0, k1, k2, k3, v0, v1, v2, v3, kt_s,
    t1, t2, t3,
    ck, cv, ak, av,
    sk1, sk2, sk3, sv1, sv2, sv3, rk1, rk2, rk3, rv1, rv2, rv3,
    load_sem, fsend, frecv, rsend, rrecv, tsend, trecv, osem,
):
    rows, dh = k0.shape
    half = rows // 2
    scale = dh ** (-0.5)
    me = lax.axis_index("ctx")
    even = lax.rem(me, 2) == 0
    sibling = me + 1 - 2 * lax.rem(me, 2)

    def at(shift):
        return lax.rem(me + shift + count, count)

    loads = [
        pltpu.make_async_copy(src, dst, load_sem.at[i])
        for i, (src, dst) in enumerate(
            [(k_hbm, k0), (v_hbm, v0), (q_hbm, q_s), (g_hbm, g_s), (o_hbm, o_s), (l_hbm, l_s)]
        )
    ]
    for copy in loads:
        copy.start()

    barrier = pltpu.get_barrier_semaphore()
    for shift in (1, 2, 3, -1, -2, -3):
        pl.semaphore_signal(barrier, inc=1, device_id=(at(shift),), device_id_type=MESH)
    pl.semaphore_wait(barrier, 6)

    def remote(src, dst, ssem, rsem, target):
        return pltpu.make_async_remote_copy(
            src_ref=src, dst_ref=dst, send_sem=ssem, recv_sem=rsem,
            device_id=(target,), device_id_type=MESH,
        )

    tags = [remote(tile_ref, t, tsend.at[i], trecv.at[i], at(i + 1)) for i, t in enumerate((t1, t2, t3))]
    send1 = [remote(k_hbm, k1, fsend.at[0], frecv.at[0], at(1)),
             remote(v_hbm, v1, fsend.at[1], frecv.at[1], at(1))]
    send3 = [remote(k_hbm, k3, fsend.at[4], frecv.at[4], at(3)),
             remote(v_hbm, v3, fsend.at[5], frecv.at[5], at(3))]
    relay_even = [remote(k1, k2, fsend.at[2], frecv.at[2], sibling),
                  remote(v1, v2, fsend.at[3], frecv.at[3], sibling)]
    relay_odd = [remote(k3, k2, fsend.at[2], frecv.at[2], sibling),
                 remote(v3, v2, fsend.at[3], frecv.at[3], sibling)]
    for copy in tags + send1 + send3:
        copy.start()

    for copy in loads:
        copy.wait()

    def grads(qh, gh, lh, dh_row, kk, vv, kt, mask):
        s = dot_nt(kk, qh)
        p = jnp.exp2(s * (scale * LOG2E) - lh)
        if mask is not None:
            p = jnp.where(mask, p, 0.0)
        dp = dot_nt(vv, gh)
        ds = (p * (dp - dh_row)).astype(BF16)
        return dot_nn(kt, ds), dot_nn(ds, qh), dot_nn(p.astype(BF16), gh)

    def transposed(ref):
        kt_s[...] = ref[...].astype(F32).T.astype(BF16)

    def operands(h, off):
        cols = pl.ds(pl.multiple_of(h * dh, dh), dh)
        part = pl.ds(off, half)
        return (q_s[part, cols], g_s[part, cols],
                l_s[pl.ds(h, 1), part] * LOG2E, d_s[h, 0:1, part])

    ck[...] = jnp.zeros_like(ck)
    cv[...] = jnp.zeros_like(cv)
    transposed(k0)
    lower, upper = slice(0, half), slice(half, rows)
    diagonal = (lax.broadcasted_iota(jnp.int32, (half, half), 0)
                <= lax.broadcasted_iota(jnp.int32, (half, half), 1))

    def own_step(h, _):
        cols = pl.ds(pl.multiple_of(h * dh, dh), dh)
        prod = g_s[:, cols].astype(F32) * o_s[:, cols].astype(F32)
        high = prod.astype(BF16)
        low = (prod - high.astype(F32)).astype(BF16)
        ones = jnp.ones((8, dh), BF16)
        d_s[h] = dot_nt(ones, high) + dot_nt(ones, low)
        ops_l, ops_u = operands(h, 0), operands(h, half)
        a = grads(*ops_u, k0[lower], v0[lower], kt_s[:, lower], None)
        b = grads(*ops_u, k0[upper], v0[upper], kt_s[:, upper], diagonal)
        c = grads(*ops_l, k0[lower], v0[lower], kt_s[:, lower], diagonal)
        dq_s[h, :, upper] = a[0] + b[0]
        dq_s[h, :, lower] = c[0]
        ck[lower] += a[1] + c[1]
        ck[upper] += b[1]
        cv[lower] += a[2] + c[2]
        cv[upper] += b[2]
        return 0

    lax.fori_loop(0, heads, own_step, 0, unroll=UNROLL)

    def visit(kx, vx, tag, tag_ref, sk, sv):
        tag.wait_recv()
        keep = (tag_ref[0:1, :] < tile_ref[0:1, :]).astype(jnp.int32).astype(F32)
        drop = 1.0 - keep
        keep_wide, drop_wide = jnp.concatenate([keep] * (half // dh), 1), jnp.concatenate([drop] * (half // dh), 1)
        keep_b, drop_b = keep.astype(BF16), drop.astype(BF16)
        keep_w, drop_w = keep_wide.astype(BF16), drop_wide.astype(BF16)
        transposed(kx)
        ak[...] = jnp.zeros_like(ak)
        av[...] = jnp.zeros_like(av)
        k_pick = kx[lower] * keep_b + kx[upper] * drop_b
        v_pick = vx[lower] * keep_b + vx[upper] * drop_b
        kt_pick = kt_s[:, lower] * keep_w + kt_s[:, upper] * drop_w

        def step(h, _):
            q_l, g_l, l_l, d_l = operands(h, 0)
            q_u, g_u, l_u, d_u = operands(h, half)
            a = grads(q_u, g_u, l_u, d_u, kx[lower], vx[lower], kt_s[:, lower], None)
            b = grads(
                q_l * keep_b + q_u * drop_b, g_l * keep_b + g_u * drop_b,
                l_l * keep_wide + l_u * drop_wide, d_l * keep_wide + d_u * drop_wide,
                k_pick, v_pick, kt_pick, None,
            )
            dq_s[h, :, upper] += a[0] + b[0] * drop_wide
            dq_s[h, :, lower] += b[0] * keep_wide
            ak[lower] += a[1]
            ak[upper] += b[1]
            av[lower] += a[2]
            av[upper] += b[2]
            return 0

        lax.fori_loop(0, heads, step, 0, unroll=UNROLL)
        sk[lower] = (ak[lower] + ak[upper] * keep).astype(BF16)
        sk[upper] = (ak[upper] * drop).astype(BF16)
        sv[lower] = (av[lower] + av[upper] * keep).astype(BF16)
        sv[upper] = (av[upper] * drop).astype(BF16)

    def give(sk, sv, rk, rv, index, target):
        copies = [remote(sk, rk, rsend.at[2 * index], rrecv.at[2 * index], target),
                  remote(sv, rv, rsend.at[2 * index + 1], rrecv.at[2 * index + 1], target)]
        for copy in copies:
            copy.start()
        return copies

    for copy in send1:
        copy.wait_recv()

    @pl.when(even)
    def _():
        for copy in relay_even:
            copy.start()

    visit(k1, v1, tags[0], t1, sk1, sv1)
    back1 = give(sk1, sv1, rk1, rv1, 0, at(-1))

    for copy in send3:
        copy.wait_recv()

    @pl.when(jnp.logical_not(even))
    def _():
        for copy in relay_odd:
            copy.start()

    visit(k3, v3, tags[2], t3, sk3, sv3)
    back3 = give(sk3, sv3, rk3, rv3, 2, at(-3))

    for copy in relay_even:
        copy.wait_recv()
    visit(k2, v2, tags[1], t2, sk2, sv2)
    back2 = give(sk2, sv2, rk2, rv2, 1, at(-2))

    for h in range(heads):
        gq_s[:, h * dh:(h + 1) * dh] = (dq_s[h].T * scale).astype(BF16)
    store = pltpu.make_async_copy(gq_s, gq_hbm, osem)
    store.start()

    for copy in back1 + back3 + back2:
        copy.wait_recv()
    gk_ref[...] = ((ck[...] + rk1[...].astype(F32) + rk2[...].astype(F32) + rk3[...].astype(F32))
                   * scale).astype(BF16)
    gv_ref[...] = (cv[...] + rv1[...].astype(F32) + rv2[...].astype(F32)
                   + rv3[...].astype(F32)).astype(BF16)

    for copy in tags + send1 + send3 + relay_even + back1 + back2 + back3:
        copy.wait_send()
    store.wait()


def on_device(queries, key_rows, value_rows, grad_out, attn_out, log_total, block_pair):
    rows, dh = key_rows.shape
    width = queries.shape[1]
    heads = width // dh
    count = lax.axis_size("ctx")
    tile = jnp.broadcast_to(block_pair.reshape(1, 1), (8, 128))
    vm = functools.partial(pltpu.VMEM)
    kv = vm((rows, dh), BF16)
    acc = vm((rows, dh), F32)
    wide = vm((rows, width), BF16)
    dma = pltpu.SemaphoreType.DMA
    any_spec = pl.BlockSpec(memory_space=pl.ANY)
    vmem_spec = pl.BlockSpec(memory_space=pltpu.VMEM)
    return tuple(pl.pallas_call(
        functools.partial(kernel, count, heads),
        out_shape=(
            jax.ShapeDtypeStruct((rows, width), BF16),
            jax.ShapeDtypeStruct((rows, dh), BF16),
            jax.ShapeDtypeStruct((rows, dh), BF16),
        ),
        in_specs=[vmem_spec] + [any_spec] * 6,
        out_specs=(any_spec, vmem_spec, vmem_spec),
        scratch_shapes=[
            wide, wide, wide, vm((heads, rows), F32), vm((heads, 8, rows), F32),
            vm((heads, dh, rows), F32), wide,
            *[kv] * 8, vm((dh, rows), BF16),
            *[vm((8, 128), jnp.int32)] * 3,
            *[acc] * 4,
            *[kv] * 12,
            dma((6,)), dma((6,)), dma((6,)), dma((6,)), dma((6,)),
            dma((3,)), dma((3,)), dma,
        ],
        compiler_params=pltpu.CompilerParams(
            collective_id=0, has_side_effects=True, vmem_limit_bytes=48 * 1024 * 1024,
        ),
        cost_estimate=pl.CostEstimate(flops=6 * 10**9, bytes_accessed=6 * 2**20, transcendentals=5 * 10**6),
    )(tile, queries, key_rows, value_rows, grad_out, attn_out, log_total))


def solution(mesh):
    return jax.shard_map(
        on_device,
        mesh=mesh,
        in_specs=(
            P("ctx", None),
            P("ctx", None),
            P("ctx", None),
            P("ctx", None),
            P("ctx", None),
            P(None, "ctx"),
            P("ctx"),
        ),
        out_specs=(P("ctx", None), P("ctx", None), P("ctx", None)),
        check_vma=False,
    )
```

time: 134 us -> 48.2 us (0.36)
  waiting for transfers between devices: 39.4 us -> 0 us
  Pallas kernels: 0 us -> 38.1 us
  matrix products: 28.3 us -> 0 us
  local copies, waits for them, and re-layouts: 33.5 us -> 8.48 us
  other arithmetic: 21 us -> 0 us
  starting transfers between devices: 7.25 us -> 0 us
  between operations: 3.66 us -> 1.31 us
    ppermute x17 -> x0, waiting for transfers between devices: 39.4 us -> none  [passed_along(): return lax.ppermute(value, axis, pairs)]
    pallas_call x0 -> x1, Pallas kernels: none -> 38.1 us  [on_device(): pl.pallas_call(functools.partial(kernel, count, heads), out_shape=(jax.Sh...]
    dot_general x20 -> x0, matrix products: 28.3 us -> none  [the longest x4 7.45 us: grad_tiles(): jnp.einsum('thqk,tqhd->tkd', probs_b, grad_in, preferred_element_type=jnp...]
    select_n x3 -> x0, local copies, waits for them, and re-layouts: 7.62 us -> none  [select_partial(): query_lower = jnp.where(earlier, grad_query[1], query_zero)]
    add x3 -> x0, local copies, waits for them, and re-layouts: 7.61 us -> none  [select_partial(): query_upper = grad_query[0] + jnp.where(earlier, query_zero, grad_query[1])]
    select_n x6 -> x0, other arithmetic: 7.28 us -> none  [the longest x3 4.62 us: select_partial(): query_lower = jnp.where(earlier, grad_query[1], query_zero)]
    ppermute x17 -> x0, starting transfers between devices: 7.25 us -> none  [passed_along(): return lax.ppermute(value, axis, pairs)]
    add x11 -> x0, other arithmetic: 6.55 us -> none  [the longest x4 2.73 us: on_device(): carried_sums = (carried_sums[0] + key_part, carried_sums[1] + value_part)]
  transfers between devices with their start and end apart: 17 -> 0, of which waited for: 6 -> 0; matrix products, arithmetic and copies ran while one was open for 60% -> 0% of each run, Pallas kernels for 0% -> 0%
where the time goes in v1:
time: 48.2 us; the launch traced here: 47.9 us
  Pallas kernels  38.1 us (79%)
  local copies, waits for them, and re-layouts  8.48 us (18%)
  between operations  1.31 us (3%)
    pallas_call x1, Pallas kernels, on_device(): pl.pallas_call(functools.partial(kernel, count, heads), out_shape=(jax.Sh...  38.1 us
    unnamed x15, local copies, waits for them, and re-layouts  8.47 us

profile of v1, /device:TPU:0, one launch (start us, length us, event | category | flops | bytes accessed | tf_op | source)
XLA Modules:
  0.0 47.9 jit_solution(13377733651387587417)
XLA Ops:
  1.3 0.0 copy-start
  1.3 1.2 %copy-done = bf16[512,1024]{1,0:T(8,128)(2,1)S(1)} copy-done((bf16[512,1024]{1,0:T(8,128)(2,1)S(1)}, bf16[512,1024]{1,0:T(8,128)(2,1)}, u32[]{:S(2)}) %copy-start) | copy-done | bytes 1048600
  2.5 0.0 copy-start.1
  2.5 1.2 %copy-done.1 = bf16[512,1024]{1,0:T(8,128)(2,1)S(1)} copy-done((bf16[512,1024]{1,0:T(8,128)(2,1)S(1)}, bf16[512,1024]{1,0:T(8,128)(2,1)}, u32[]{:S(2)}) %copy-start.1) | copy-done | bytes 1048600
  3.7 0.0 copy-start.2
  3.7 1.2 %copy-done.2 = bf16[512,1024]{1,0:T(8,128)(2,1)S(1)} copy-done((bf16[512,1024]{1,0:T(8,128)(2,1)S(1)}, bf16[512,1024]{1,0:T(8,128)(2,1)}, u32[]{:S(2)}) %copy-start.2) | copy-done | bytes 1048600
  5.0 0.0 copy-start.3
  5.0 0.9 %copy-done.3 = bf16[512,128]{1,0:T(8,128)(2,1)S(1)} copy-done((bf16[512,128]{1,0:T(8,128)(2,1)S(1)}, bf16[512,128]{1,0:T(8,128)(2,1)}, u32[]{:S(2)}) %copy-start.3) | copy-done | bytes 131096
  5.9 0.0 copy-start.4
  5.9 0.9 %copy-done.4 = bf16[512,128]{1,0:T(8,128)(2,1)S(1)} copy-done((bf16[512,128]{1,0:T(8,128)(2,1)S(1)}, bf16[512,128]{1,0:T(8,128)(2,1)}, u32[]{:S(2)}) %copy-start.4) | copy-done | bytes 131096
  6.8 0.0 copy-start.5
  6.8 0.7 %copy-done.5 = f32[8,512]{1,0:T(8,128)S(1)} copy-done((f32[8,512]{1,0:T(8,128)S(1)}, f32[8,512]{1,0:T(8,128)}, u32[]{:S(2)}) %copy-start.5) | copy-done | bytes 16408
  7.5 38.1 %shard_map.94 = (bf16[512,1024]{1,0:T(8,128)(2,1)S(1)}, bf16[512,128]{1,0:T(8,128)(2,1)S(1)}, bf16[512,128]{1,0:T(8,128)(2,1)S(1)}) custom-call(s32[8,128]{1,0:T(8,128)S(1)} %broadcast_in_dim.8.tile_ref, bf16[512,1024]{1,0:T(8,128)(2,1)S(1)} %copy-done, bf16[512,128]{1,0:T(8,128)(2,1)S(1)} %copy-done.3, bf16[512,128]{1,0:T(8,128)(2,1)S(1)} %copy-done.4, ...), custom_call_target="tpu_custom_call" | custom-call | flops 6000000000 | bytes 6291456 | tf_op jit(solution)/shard_map/pallas_call | solution.py:228
  45.6 1.0 %copy.14 = bf16[512,1024]{1,0:T(8,128)(2,1)} copy(bf16[512,1024]{1,0:T(8,128)(2,1)S(1)} %get-tuple-element.6) | data formatting | bytes 2097152
  46.5 0.7 %copy.15 = bf16[512,128]{1,0:T(8,128)(2,1)} copy(bf16[512,128]{1,0:T(8,128)(2,1)S(1)} %get-tuple-element.7) | data formatting | bytes 262144
  47.2 0.7 %copy.16 = bf16[512,128]{1,0:T(8,128)(2,1)} copy(bf16[512,128]{1,0:T(8,128)(2,1)S(1)} %get-tuple-element.8) | data formatting | bytes 262144
  (1 shorter events, 0.0 us)
Async XLA Ops:
  1.3 1.2 %copy-start = (bf16[512,1024]{1,0:T(8,128)(2,1)S(1)}, bf16[512,1024]{1,0:T(8,128)(2,1)}, u32[]{:S(2)}) copy-start(bf16[512,1024]{1,0:T(8,128)(2,1)} %q_hbm.1) | copy-start | bytes 3145732
  2.5 1.2 %copy-start.1 = (bf16[512,1024]{1,0:T(8,128)(2,1)S(1)}, bf16[512,1024]{1,0:T(8,128)(2,1)}, u32[]{:S(2)}) copy-start(bf16[512,1024]{1,0:T(8,128)(2,1)} %g_hbm.1) | copy-start | bytes 3145732
  3.7 1.2 %copy-start.2 = (bf16[512,1024]{1,0:T(8,128)(2,1)S(1)}, bf16[512,1024]{1,0:T(8,128)(2,1)}, u32[]{:S(2)}) copy-start(bf16[512,1024]{1,0:T(8,128)(2,1)} %o_hbm.1) | copy-start | bytes 3145732
  5.0 0.9 %copy-start.3 = (bf16[512,128]{1,0:T(8,128)(2,1)S(1)}, bf16[512,128]{1,0:T(8,128)(2,1)}, u32[]{:S(2)}) copy-start(bf16[512,128]{1,0:T(8,128)(2,1)} %k_hbm.1) | copy-start | bytes 393220
  5.9 0.9 %copy-start.4 = (bf16[512,128]{1,0:T(8,128)(2,1)S(1)}, bf16[512,128]{1,0:T(8,128)(2,1)}, u32[]{:S(2)}) copy-start(bf16[512,128]{1,0:T(8,128)(2,1)} %v_hbm.1) | copy-start | bytes 393220
  6.8 0.7 %copy-start.5 = (f32[8,512]{1,0:T(8,128)S(1)}, f32[8,512]{1,0:T(8,128)}, u32[]{:S(2)}) copy-start(f32[8,512]{1,0:T(8,128)} %l_hbm.1) | copy-start | bytes 49156

commit v2 on v1

--- a/solution.py
+++ b/solution.py
@@ -12,7 +12,7 @@
 LOG2E = math.log2(math.e)
 F32 = jnp.float32
 BF16 = jnp.bfloat16
-UNROLL = 2
+UNROLL = 4
 
 
 def dot_nt(a, b):
@@ -245,7 +245,7 @@
             dma((3,)), dma((3,)), dma,
         ],
         compiler_params=pltpu.CompilerParams(
-            collective_id=0, has_side_effects=True, vmem_limit_bytes=48 * 1024 * 1024,
+            collective_id=0, has_side_effects=True, vmem_limit_bytes=62 * 1024 * 1024,
         ),
         cost_estimate=pl.CostEstimate(flops=6 * 10**9, bytes_accessed=6 * 2**20, transcendentals=5 * 10**6),
     )(tile, queries, key_rows, value_rows, grad_out, attn_out, log_total))

time: 48.2 us -> 44.4 us (0.921)
  local copies, waits for them, and re-layouts: 8.48 us -> 4.5 us
    unnamed x15 -> x7, local copies, waits for them, and re-layouts: 8.47 us -> 3.91 us
    broadcast_in_dim x1, local copies, waits for them, and re-layouts: 0.01 us -> 0.59 us  [on_device(): tile = jnp.broadcast_to(block_pair.reshape(1, 1), (8, 128))]
where the time goes in v2:
time: 44.4 us; the launch traced here: 44.2 us
  Pallas kernels  38.4 us (86%)
  local copies, waits for them, and re-layouts  4.5 us (10%)
  between operations  1.3 us (3%)
    pallas_call x1, Pallas kernels, on_device(): pl.pallas_call(functools.partial(kernel, count, heads), out_shape=(jax.Sh...  38.4 us
    unnamed x7, local copies, waits for them, and re-layouts  3.91 us

profile of v2, /device:TPU:0, one launch (start us, length us, event | category | flops | bytes accessed | tf_op | source)
XLA Modules:
  0.0 44.2 jit_solution(13098262664136723871)
XLA Ops:
  1.3 0.6 %broadcast_in_dim.8.tile_ref = s32[8,128]{1,0:T(8,128)} broadcast(s32[]{:T(128)} %bitcast.1), dimensions={} | broadcast | bytes 4100 | tf_op jit(solution)/shard_map/broadcast_in_dim | solution.py:220
  1.9 38.4 %shard_map.94 = (bf16[512,1024]{1,0:T(8,128)(2,1)}, bf16[512,128]{1,0:T(8,128)(2,1)}, bf16[512,128]{1,0:T(8,128)(2,1)}) custom-call(s32[8,128]{1,0:T(8,128)} %broadcast_in_dim.8.tile_ref, bf16[512,1024]{1,0:T(8,128)(2,1)} %q_hbm.1, bf16[512,128]{1,0:T(8,128)(2,1)} %k_hbm.1, bf16[512,128]{1,0:T(8,128)(2,1)} %v_hbm.1, bf16[512,1024]{1,0:T(8,128)(2,1)} %g_hbm.1, ...), custom_call_target="tpu_custom_call" | custom-call | flops 6000000000 | bytes 6291456 | tf_op jit(solution)/shard_map/pallas_call | solution.py:228
  40.2 0.0 copy-start.1
  40.3 2.3 %copy.14 = bf16[512,1024]{1,0:T(8,128)(2,1)} copy(bf16[512,1024]{1,0:T(8,128)(2,1)} %get-tuple-element.6) | data formatting | bytes 2097152
  42.6 0.0 copy-done.1
  42.6 0.0 copy-start
  42.6 0.7 %copy.15 = bf16[512,128]{1,0:T(8,128)(2,1)} copy(bf16[512,128]{1,0:T(8,128)(2,1)S(1)} %copy-done.1) | data formatting | bytes 262144
  43.2 0.3 copy-done
  43.5 0.7 %copy.16 = bf16[512,128]{1,0:T(8,128)(2,1)} copy(bf16[512,128]{1,0:T(8,128)(2,1)S(1)} %copy-done) | data formatting | bytes 262144
Async XLA Ops:
  40.2 2.3 %copy-start.1 = (bf16[512,128]{1,0:T(8,128)(2,1)S(1)}, bf16[512,128]{1,0:T(8,128)(2,1)}, u32[]{:S(2)}) copy-start(bf16[512,128]{1,0:T(8,128)(2,1)} %get-tuple-element.7) | copy-start | bytes 393220
  42.6 1.0 %copy-start = (bf16[512,128]{1,0:T(8,128)(2,1)S(1)}, bf16[512,128]{1,0:T(8,128)(2,1)}, u32[]{:S(2)}) copy-start(bf16[512,128]{1,0:T(8,128)(2,1)} %get-tuple-element.8) | copy-start | bytes 393220

commit v3 on v2

--- a/solution.py
+++ b/solution.py
@@ -72,7 +72,7 @@
                   remote(v1, v2, fsend.at[3], frecv.at[3], sibling)]
     relay_odd = [remote(k3, k2, fsend.at[2], frecv.at[2], sibling),
                  remote(v3, v2, fsend.at[3], frecv.at[3], sibling)]
-    for copy in tags + send1 + send3:
+    for copy in send3 + send1 + tags:
         copy.start()
 
     for copy in loads:

time: 44.4 us -> 46.1 us (1.038)
  Pallas kernels: 38.4 us -> 40.1 us
    pallas_call x1, Pallas kernels: 38.4 us -> 40.1 us  [on_device(): pl.pallas_call(functools.partial(kernel, count, heads), out_shape=(jax.Sh...]
where the time goes in v3:
time: 46.1 us; the launch traced here: 45.9 us
  Pallas kernels  40.1 us (87%)
  local copies, waits for them, and re-layouts  4.5 us (10%)
  between operations  1.3 us (3%)
    pallas_call x1, Pallas kernels, on_device(): pl.pallas_call(functools.partial(kernel, count, heads), out_shape=(jax.Sh...  40.1 us
    unnamed x7, local copies, waits for them, and re-layouts  3.91 us

profile of v3, /device:TPU:0, one launch (start us, length us, event | category | flops | bytes accessed | tf_op | source)
XLA Modules:
  0.0 45.9 jit_solution(7845538191499847113)
XLA Ops:
  1.3 0.6 %broadcast_in_dim.8.tile_ref = s32[8,128]{1,0:T(8,128)} broadcast(s32[]{:T(128)} %bitcast.1), dimensions={} | broadcast | bytes 4100 | tf_op jit(solution)/shard_map/broadcast_in_dim | solution.py:220
  1.9 40.1 %shard_map.94 = (bf16[512,1024]{1,0:T(8,128)(2,1)}, bf16[512,128]{1,0:T(8,128)(2,1)}, bf16[512,128]{1,0:T(8,128)(2,1)}) custom-call(s32[8,128]{1,0:T(8,128)} %broadcast_in_dim.8.tile_ref, bf16[512,1024]{1,0:T(8,128)(2,1)} %q_hbm.1, bf16[512,128]{1,0:T(8,128)(2,1)} %k_hbm.1, bf16[512,128]{1,0:T(8,128)(2,1)} %v_hbm.1, bf16[512,1024]{1,0:T(8,128)(2,1)} %g_hbm.1, ...), custom_call_target="tpu_custom_call" | custom-call | flops 6000000000 | bytes 6291456 | tf_op jit(solution)/shard_map/pallas_call | solution.py:228
  42.0 0.0 copy-start.1
  42.0 2.3 %copy.14 = bf16[512,1024]{1,0:T(8,128)(2,1)} copy(bf16[512,1024]{1,0:T(8,128)(2,1)} %get-tuple-element.6) | data formatting | bytes 2097152
  44.3 0.0 copy-done.1
  44.3 0.0 copy-start
  44.3 0.7 %copy.15 = bf16[512,128]{1,0:T(8,128)(2,1)} copy(bf16[512,128]{1,0:T(8,128)(2,1)S(1)} %copy-done.1) | data formatting | bytes 262144
  44.9 0.3 copy-done
  45.2 0.7 %copy.16 = bf16[512,128]{1,0:T(8,128)(2,1)} copy(bf16[512,128]{1,0:T(8,128)(2,1)S(1)} %copy-done) | data formatting | bytes 262144
Async XLA Ops:
  42.0 2.3 %copy-start.1 = (bf16[512,128]{1,0:T(8,128)(2,1)S(1)}, bf16[512,128]{1,0:T(8,128)(2,1)}, u32[]{:S(2)}) copy-start(bf16[512,128]{1,0:T(8,128)(2,1)} %get-tuple-element.7) | copy-start | bytes 393220
  44.3 1.0 %copy-start = (bf16[512,128]{1,0:T(8,128)(2,1)S(1)}, bf16[512,128]{1,0:T(8,128)(2,1)}, u32[]{:S(2)}) copy-start(bf16[512,128]{1,0:T(8,128)(2,1)} %get-tuple-element.8) | copy-start | bytes 393220
